TPU v7x, 512 devices: a whole 4x4x16 slice. The times are simulated.
512 devices in a mesh: seq: 32 (over z_hi, x, core), dp: 16 (over y, z_lo).
Axes of the slice: x: 4, y: 4, z: 16 (z_hi: 4, z_lo: 4; z = z_hi * 4 + z_lo), core: 2. Of those that a mesh axis runs over, the one named last changes fastest.
Arguments:
- queries: bfloat16 [2048, 32, 1024], P('seq', 'dp'), may hold values from -12 to 12
- key_vectors: bfloat16 [2048, 32, 1024], P('seq', 'dp'), may hold values from -12 to 12
- value_vectors: bfloat16 [2048, 32, 1024], P('seq', 'dp'), may hold values from -6 to 6
- features: bfloat16 [2048, 32, 1024], P('seq', 'dp'), may hold values from -6 to 6
- cotangent: bfloat16 [2048, 32, 1024], P('seq', 'dp'), may hold values from -6 to 6
- frames: int32 [32], P('dp'), may hold values from 512 to 2048, as said below
- conv_kernel: float32 [31, 1024], replicated, may hold values from -1 to 1
- conv_bias: float32 [1024], replicated, may hold values from -3 to 3
Outputs:
- block_out: bfloat16 [2048, 32, 1024], P('seq', 'dp')
- grad_features: bfloat16 [2048, 32, 1024], P('seq', 'dp')
- grad_queries: bfloat16 [2048, 32, 1024], P('seq', 'dp')
- grad_keys: bfloat16 [2048, 32, 1024], P('seq', 'dp')
- grad_values: bfloat16 [2048, 32, 1024], P('seq', 'dp')
- grad_kernel: float32 [31, 1024], replicated
- grad_bias: float32 [1024], replicated
Inputs may be any that keep to these rules, and one draw needn't show every extreme that they name: Every utterance has at least 512 valid frames, and utterance 0 has all 2048.
All inputs are finite; a program needn't handle non-finite values.
Results may differ from a plain program's by a relative error of at most 0.0065.
Values may be sent and summed in bfloat16 or wider, within the bound.
No kernel may reach another device: no remote copies, remote signals or barrier semaphores. Data moves between devices by JAX's collectives and lax.ppermute only.
A program may use at most 64 MiB of HBM per device.

v0:
```python
import math
import jax
import jax.numpy as jnp
from jax import lax
from jax.sharding import PartitionSpec as P

HEADS = 16
TAPS = 31


def extended(block, sides, width):
    for axis, dim in sides:
        count = lax.axis_size(axis)
        forward = [(i, i + 1) for i in range(count - 1)]
        backward = [(target, source) for source, target in forward]
        low = lax.ppermute(
            lax.slice_in_dim(block, block.shape[dim] - width, None, axis=dim), axis, forward
        )
        high = lax.ppermute(lax.slice_in_dim(block, 0, width, axis=dim), axis, backward)
        block = jnp.concatenate([low, block, high], axis=dim)
    return block


def to_heads(stacked):
    return lax.all_to_all(stacked, "seq", split_axis=1, concat_axis=0, tiled=True)


def to_frames(stacked):
    return lax.all_to_all(stacked, "seq", split_axis=0, concat_axis=1, tiled=True)


def conv_rim(field):
    return extended(field, (("seq", 0),), TAPS // 2)


def block_probs(query_block, key_rows, key_count):
    score_scale = 1.0 / math.sqrt(key_rows.shape[1])
    scores = (
        jnp.einsum("qd,kd->qk", query_block, key_rows, preferred_element_type=jnp.float32)
        * score_scale
    )
    allowed = jnp.arange(key_rows.shape[0]) < key_count
    scores = jnp.where(allowed[None, :], scores, -jnp.inf)
    row_max = jnp.max(scores, axis=1, keepdims=True)
    exp_scores = jnp.exp(scores - row_max)
    return exp_scores / jnp.sum(exp_scores, axis=1, keepdims=True)


def attend_forward(query_rows, key_rows, value_rows, key_count):
    seq_len = query_rows.shape[0]
    block_rows = min(512, seq_len)

    def one_block(block_index):
        query_block = lax.dynamic_slice_in_dim(query_rows, block_index * block_rows, block_rows, 0)
        probs_bf = block_probs(query_block, key_rows, key_count).astype(jnp.bfloat16)
        return jnp.dot(probs_bf, value_rows, preferred_element_type=jnp.float32).astype(
            jnp.bfloat16
        )

    outputs = lax.map(one_block, jnp.arange(seq_len // block_rows))
    return outputs.reshape(seq_len, query_rows.shape[1])


def attend_backward(query_rows, key_rows, value_rows, grad_out, key_count):
    seq_len, head_dim = query_rows.shape
    block_rows = min(512, seq_len)
    score_scale = 1.0 / math.sqrt(head_dim)

    def one_block(totals, block_index):
        grad_key_acc, grad_val_acc = totals
        first_row = block_index * block_rows
        query_block = lax.dynamic_slice_in_dim(query_rows, first_row, block_rows, 0)
        grad_block = lax.dynamic_slice_in_dim(grad_out, first_row, block_rows, 0)
        probs = block_probs(query_block, key_rows, key_count)
        probs_bf = probs.astype(jnp.bfloat16)
        grad_probs = jnp.einsum(
            "qd,kd->qk", grad_block, value_rows, preferred_element_type=jnp.float32
        )
        grad_val_acc = grad_val_acc + jnp.einsum(
            "qk,qd->kd", probs_bf, grad_block, preferred_element_type=jnp.float32
        )
        row_delta = jnp.sum(probs * grad_probs, axis=1, keepdims=True)
        grad_scores = (probs * (grad_probs - row_delta) * score_scale).astype(jnp.bfloat16)
        grad_query = jnp.dot(grad_scores, key_rows, preferred_element_type=jnp.float32).astype(
            jnp.bfloat16
        )
        grad_key_acc = grad_key_acc + jnp.einsum(
            "qk,qd->kd", grad_scores, query_block, preferred_element_type=jnp.float32
        )
        return ((grad_key_acc, grad_val_acc), grad_query)

    zero_rows = jnp.zeros((seq_len, head_dim), jnp.float32)
    final, grad_queries = lax.scan(
        one_block, (zero_rows, zero_rows), jnp.arange(seq_len // block_rows)
    )
    return (
        grad_queries.reshape(seq_len, head_dim),
        final[0].astype(jnp.bfloat16),
        final[1].astype(jnp.bfloat16),
    )


def depthwise(padded, kernel, row_count, reverse_taps):
    result = None
    for tap_index in range(TAPS):
        offset = TAPS - 1 - tap_index if reverse_taps else tap_index
        tap_term = kernel[tap_index] * lax.slice_in_dim(
            padded, offset, offset + row_count, axis=0
        ).astype(jnp.float32)
        result = tap_term if tap_index == 0 else result + tap_term
    return result


def conv_module(hidden, valid_rows, kernel, bias, cotangent, pad_field):
    row_count = hidden.shape[0]
    lead_axes = tuple(range(hidden.ndim - 1))
    masked = jnp.where(valid_rows, hidden, 0.0).astype(jnp.bfloat16)
    padded = pad_field(masked)
    conv_out = bias + depthwise(padded, kernel, row_count, False)
    gate_value = jax.nn.sigmoid(conv_out)
    block_out = (hidden + conv_out * gate_value).astype(jnp.bfloat16)
    cot_rows = cotangent.astype(jnp.float32)
    grad_conv = cot_rows * gate_value * (1.0 + conv_out * (1.0 - gate_value))
    grad_padded = pad_field(grad_conv.astype(jnp.bfloat16))
    grad_masked = depthwise(grad_padded, kernel, row_count, True)
    grad_features = (cot_rows + jnp.where(valid_rows, grad_masked, 0.0)).astype(jnp.bfloat16)
    grad_kernel = jnp.stack(
        [
            jnp.sum(
                grad_conv
                * lax.slice_in_dim(padded, tap_index, tap_index + row_count, axis=0).astype(
                    jnp.float32
                ),
                axis=lead_axes,
            )
            for tap_index in range(TAPS)
        ]
    )
    grad_bias = jnp.sum(grad_conv, axis=lead_axes)
    return (block_out, grad_features, grad_kernel, grad_bias)


def on_device(
    queries, key_vectors, value_vectors, features, cotangent, frames, conv_kernel, conv_bias
):
    local_len, utt_local, model_width = queries.shape
    head_dim = model_width // HEADS
    item_total = utt_local * HEADS
    seq_devices = lax.axis_size("seq")
    item_count = item_total // seq_devices
    item_ids = lax.axis_index("seq") * item_count + jnp.arange(item_count)
    item_utt = item_ids // HEADS
    item_frames = jnp.sum(
        jnp.where(item_utt[:, None] == jnp.arange(utt_local)[None, :], frames[None, :], 0), axis=1
    )

    def by_items(field):
        return field.reshape(local_len, item_total, head_dim)

    def from_items(field):
        return field.reshape(local_len, utt_local, model_width)

    stacked = jnp.concatenate(
        (by_items(queries), by_items(key_vectors), by_items(value_vectors)), axis=2
    )
    arrived = to_heads(stacked)

    def forward_item(item_index):
        packed = lax.dynamic_index_in_dim(arrived, item_index, 1, keepdims=False)
        return attend_forward(
            packed[:, :head_dim],
            packed[:, head_dim : 2 * head_dim],
            packed[:, 2 * head_dim :],
            item_frames[item_index],
        )

    context = lax.map(forward_item, jnp.arange(item_count))
    context = from_items(to_frames(jnp.moveaxis(context, 0, 1)))
    hidden = features.astype(jnp.float32) + context.astype(jnp.float32)
    positions = lax.axis_index("seq") * local_len + jnp.arange(local_len)
    valid_rows = (positions[:, None] < frames[None, :])[:, :, None]
    block_out, grad_features, grad_kernel, grad_bias = conv_module(
        hidden, valid_rows, conv_kernel, conv_bias, cotangent, conv_rim
    )
    grad_arrived = to_heads(by_items(grad_features))

    def backward_item(item_index):
        packed = lax.dynamic_index_in_dim(arrived, item_index, 1, keepdims=False)
        grad_out = lax.dynamic_index_in_dim(grad_arrived, item_index, 1, keepdims=False)
        grad_triple = attend_backward(
            packed[:, :head_dim],
            packed[:, head_dim : 2 * head_dim],
            packed[:, 2 * head_dim :],
            grad_out,
            item_frames[item_index],
        )
        return jnp.concatenate(grad_triple, axis=1)

    grad_rows = lax.map(backward_item, jnp.arange(item_count))
    grad_rows = to_frames(jnp.moveaxis(grad_rows, 0, 1))
    grad_queries = from_items(grad_rows[:, :, :head_dim])
    grad_keys = from_items(grad_rows[:, :, head_dim : 2 * head_dim])
    grad_values = from_items(grad_rows[:, :, 2 * head_dim :])
    grad_kernel, grad_bias = lax.psum((grad_kernel, grad_bias), ("seq", "dp"))
    return (block_out, grad_features, grad_queries, grad_keys, grad_values, grad_kernel, grad_bias)


def solution(mesh):
    return jax.shard_map(
        on_device,
        mesh=mesh,
        in_specs=(
            P("seq", "dp", None),
            P("seq", "dp", None),
            P("seq", "dp", None),
            P("seq", "dp", None),
            P("seq", "dp", None),
            P("dp"),
            P(),
            P(),
        ),
        out_specs=(
            P("seq", "dp", None),
            P("seq", "dp", None),
            P("seq", "dp", None),
            P("seq", "dp", None),
            P("seq", "dp", None),
            P(),
            P(),
        ),
        check_vma=False,
    )
```

profile of v0, /device:TPU:1, one launch (start us, length us, event | category | flops | bytes accessed | tf_op | source)
XLA Modules:
  0.0 755.6 jit_solution(1275026097187744903)
XLA Ops:
  7.2 1.3 reshape.143
  8.7 1.3 reshape.144
  10.3 1.3 reshape.145
  11.8 1.5 pad_maximum_fusion
  13.3 19.2 %all-to-all-start = ((bf16[64,32,192]{2,0,1:T(8,128)(2,1)}), bf16[64,32,192]{2,0,1:T(8,128)(2,1)S(1)}, u32[]{:S(2)}, u32[]{:S(2)}) async-start(bf16[64,32,192]{2,0,1:T(8,128)(2,1)} %pad_maximum_fusion), calls=%async_computation | async-start | bytes 2097152 | tf_op jit(solution)/shard_map/all_to_all | solution.py:25
  33.2 52.1 %all-to-all-done = bf16[64,32,192]{2,0,1:T(8,128)(2,1)S(1)} async-done(((bf16[64,32,192]{2,0,1:T(8,128)(2,1)}), bf16[64,32,192]{2,0,1:T(8,128)(2,1)S(1)}, u32[]{:S(2)}, u32[]{:S(2)}) %all-to-all-start) | async-done | bytes 786464 | tf_op jit(solution)/shard_map/all_to_all | solution.py:25
  85.7 19.7 %while.41 = (s32[]{:T(128)}, bf16[4,512,64]{1,2,0:T(8,128)(2,1)S(1)}, s32[]{:T(128)}, s32[4]{0:T(128)S(1)}, bf16[2048,64]{1,0:T(8,128)(2,1)S(1)}, /*index=5*/bf1...) while((s32[]{:T(128)}, ...), condition=%wide.region_4.5_spmd, body=%wide.region_1.4_spmd.sunk | while | flops 281052160 | bytes 13846715 | solution.py:60
  89.4 1.3 fusion.184
  94.3 1.3 fusion.184
  99.2 1.3 fusion.184
  107.3 11.6 %reduce.2 = bf16[2048,64]{1,0:T(8,128)(2,1)S(1)} reduce(bf16[2048,1,64]{2,1,0:T(2,128)(2,1)S(1)} %reshape.153, bf16[]{:T(256)} %broadcast.102), dimensions={1}, to_apply=%reshape.153.reduce_sub_computation | reduce | bytes 524290 | tf_op jit(solution)/shard_map/transpose | solution.py:178
  120.0 8.1 %all-to-all-start.1 = ((bf16[32,2,2048]{2,1,0:T(2,128)(2,1)}), bf16[32,2,2048]{2,1,0:T(2,128)(2,1)S(1)}, u32[]{:S(2)}, u32[]{:S(2)}) async-start(bf16[32,2,2048]{2,1,0:T(2,128)(2,1)} %reshape.154), calls=%async_computation.1 | async-start | bytes 524288 | tf_op jit(solution)/shard_map/all_to_all | solution.py:29
  128.2 18.8 %all-to-all-done.1 = bf16[32,2,2048]{2,1,0:T(2,128)(2,1)S(1)} async-done(((bf16[32,2,2048]{2,1,0:T(2,128)(2,1)}), bf16[32,2,2048]{2,1,0:T(2,128)(2,1)S(1)}, u32[]{:S(2)}, u32[]{:S(2)}) %all-to-all-start.1) | async-done | bytes 262176 | tf_op jit(solution)/shard_map/all_to_all | solution.py:29
  148.7 2.0 copy.75
  150.7 1.7 reshape.151
  152.7 2.1 collective-permute-start
  154.8 2.2 collective-permute-start.1
  157.1 3.3 collective-permute-done.1
  160.4 5.0 fusion.89
  166.6 1.9 collective-permute-start.2
  168.5 3.6 collective-permute-start.3
  172.2 1.3 collective-permute-done.3
  173.5 3.3 fusion.91
  181.2 29.3 %all-to-all-start.2 = ((bf16[32,2,2048]{2,1,0:T(2,128)(2,1)}), bf16[32,2,2048]{2,1,0:T(2,128)(2,1)}, u32[]{:S(2)}, u32[]{:S(2)}) async-start(bf16[32,2,2048]{2,1,0:T(2,128)(2,1)} %reshape.156), calls=%async_computation.2 | async-start | bytes 524288 | tf_op jit(solution)/shard_map/all_to_all | solution.py:25
  210.5 19.9 %all-to-all-done.2 = bf16[32,2,2048]{2,1,0:T(2,128)(2,1)} async-done(((bf16[32,2,2048]{2,1,0:T(2,128)(2,1)}), bf16[32,2,2048]{2,1,0:T(2,128)(2,1)}, u32[]{:S(2)}, u32[]{:S(2)}) %all-to-all-start.2) | async-done | bytes 262176 | tf_op jit(solution)/shard_map/all_to_all | solution.py:25
  230.5 2.1 reshape.157
  233.3 40.2 %while.42 = (s32[]{:T(128)}, f32[2048,64]{0,1:T(8,128)S(1)}, f32[2048,64]{0,1:T(8,128)}, bf16[4,512,64]{1,2,0:T(8,128)(2,1)}, s32[]{:T(128)}, /*index=5*/s32[4]{...) while((s32[]{:T(128)}, f32[2048,64]{0,1:T(8,128)S(1)}, ...), condition=%wide.region_9.10_spmd.clone, body=%wide.region_5.9_spmd.clone.sunk | while | flops 698909184 | bytes 45975896 | solution.py:93
  238.3 1.4 multiply_reduce_fusion.2
  239.7 1.7 multiply_convert_fusion.2
  241.4 1.4 fusion.195
  248.3 1.4 multiply_reduce_fusion.2
  249.7 1.7 multiply_convert_fusion.2
  251.4 1.4 fusion.195
  258.4 1.4 multiply_reduce_fusion.2
  259.8 1.7 multiply_convert_fusion.2
  261.5 1.4 fusion.195
  268.4 1.4 multiply_reduce_fusion.2
  269.9 1.7 multiply_convert_fusion.2
  271.6 1.4 fusion.195
  275.7 1.9 reduce.3
  277.8 1.4 copy.103
  279.2 2.1 reshape.158
  281.3 6.0 all-to-all-start.3
  290.0 2.7 stack.127
  292.7 107.3 %psum.15 = f32[1024]{0:T(1024)} all-reduce(f32[1024]{0:T(1024)S(1)} %copy-done.25), channel_id=1, replica_groups=mesh['seq'=32,'dp'=16] {'seq','dp'}, use_global_device_ids=true, to_apply=%region_43.44 | all-reduce | flops 1024 | bytes 8192 | tf_op jit(solution)/shard_map/psum | solution.py:204
  400.0 4.5 reshape.159
  409.1 338.1 %all-reduce.2.cloned.1.call-done = f32[31,1024]{1,0:T(8,128)} async-done(((f32[31,1024]{1,0:T(8,128)}), f32[31,1024]{1,0:T(8,128)}) %all-reduce.2.cloned.1.call-update) | async-done | bytes 126992 | tf_op jit(solution)/shard_map/psum | solution.py:204
  747.2 1.6 copy.125
  (172 shorter events, 54.7 us)
Async XLA Ops:
  8.7 23.8 %copy-start.27 = (s32[2]{0:T(128)S(1)}, s32[2]{0:T(128)}, u32[]{:S(2)}) copy-start(s32[2]{0:T(128)} %param.17) | copy-start | bytes 28
  13.3 72.0 %all-to-all-start = ((bf16[64,32,192]{2,0,1:T(8,128)(2,1)}), bf16[64,32,192]{2,0,1:T(8,128)(2,1)S(1)}, u32[]{:S(2)}, u32[]{:S(2)}) async-start(bf16[64,32,192]{2,0,1:T(8,128)(2,1)} %pad_maximum_fusion), calls=%async_computation | async-start | bytes 2097152 | tf_op jit(solution)/shard_map/all_to_all | solution.py:25
  105.4 0.8 copy-start.7
  106.2 22.0 %copy-start.9 = (f32[31,1024]{1,0:T(8,128)S(1)}, f32[31,1024]{1,0:T(8,128)}, u32[]{:S(2)}) copy-start(f32[31,1024]{1,0:T(8,128)} %param.18) | copy-start | bytes 380932
  120.0 32.5 %copy-start.2 = (bf16[64,2,1024]{2,1,0:T(2,128)(2,1)S(1)}, bf16[64,2,1024]{2,1,0:T(2,128)(2,1)}, u32[]{:S(2)}) copy-start(bf16[64,2,1024]{2,1,0:T(2,128)(2,1)} %param.15) | copy-start | bytes 786436
  120.0 27.1 %all-to-all-start.1 = ((bf16[32,2,2048]{2,1,0:T(2,128)(2,1)}), bf16[32,2,2048]{2,1,0:T(2,128)(2,1)S(1)}, u32[]{:S(2)}, u32[]{:S(2)}) async-start(bf16[32,2,2048]{2,1,0:T(2,128)(2,1)} %reshape.154), calls=%async_computation.1 | async-start | bytes 524288 | tf_op jit(solution)/shard_map/all_to_all | solution.py:29
  128.2 24.3 %copy-start.26 = (pred[64,2]{0,1:T(4,128)(4,1)}, pred[64,2]{0,1:T(4,128)(4,1)S(1)}, u32[]{:S(2)}) copy-start(pred[64,2]{0,1:T(4,128)(4,1)S(1)} %broadcast_compare_fusion) | copy-start | bytes 388
  147.7 12.7 %copy-start.1 = (bf16[64,2,1024]{2,1,0:T(2,128)(2,1)S(1)}, bf16[64,2,1024]{2,1,0:T(2,128)(2,1)}, u32[]{:S(2)}) copy-start(bf16[64,2,1024]{2,1,0:T(2,128)(2,1)} %param.16) | copy-start | bytes 786436
  152.7 4.4 collective-permute-start
  154.8 5.6 collective-permute-start.1
  166.6 5.6 collective-permute-start.2
  168.5 5.0 collective-permute-start.3
  181.2 49.3 %all-to-all-start.2 = ((bf16[32,2,2048]{2,1,0:T(2,128)(2,1)}), bf16[32,2,2048]{2,1,0:T(2,128)(2,1)}, u32[]{:S(2)}, u32[]{:S(2)}) async-start(bf16[32,2,2048]{2,1,0:T(2,128)(2,1)} %reshape.156), calls=%async_computation.2 | async-start | bytes 524288 | tf_op jit(solution)/shard_map/all_to_all | solution.py:25
  235.2 1.8 copy-start.4
  235.2 1.8 copy-start.5
  237.0 1.2 copy-start.8
  238.2 1.4 copy-start.6
  245.3 1.8 copy-start.4
  245.3 1.8 copy-start.5
  247.0 1.2 copy-start.8
  248.3 1.4 copy-start.6
  255.3 1.8 copy-start.4
  255.3 1.8 copy-start.5
  257.1 1.2 copy-start.8
  258.4 1.4 copy-start.6
  265.4 1.8 copy-start.4
  265.4 1.8 copy-start.5
  267.2 1.2 copy-start.8
  268.4 1.4 copy-start.6
  275.7 11.7 %copy-start.3 = (bf16[64,2,1024]{2,1,0:T(2,128)(2,1)S(1)}, bf16[64,2,1024]{2,1,0:T(2,128)(2,1)}, u32[]{:S(2)}) copy-start(bf16[64,2,1024]{2,1,0:T(2,128)(2,1)} %param.15) | copy-start | bytes 786436
  277.7 12.2 %copy-start.10 = (f32[1024]{0:T(1024)S(1)}, f32[1024]{0:T(1024)}, u32[]{:S(2)}) copy-start(f32[1024]{0:T(1024)} %get-tuple-element.177) | copy-start | bytes 12292
  277.7 12.2 %copy-start.11 = (f32[1024]{0:T(1024)S(1)}, f32[1024]{0:T(1024)}, u32[]{:S(2)}) copy-start(f32[1024]{0:T(1024)} %get-tuple-element.178) | copy-start | bytes 12292
  277.7 12.2 %copy-start.12 = (f32[1024]{0:T(1024)S(1)}, f32[1024]{0:T(1024)}, u32[]{:S(2)}) copy-start(f32[1024]{0:T(1024)} %get-tuple-element.179) | copy-start | bytes 12292
  277.7 12.2 %copy-start.13 = (f32[1024]{0:T(1024)S(1)}, f32[1024]{0:T(1024)}, u32[]{:S(2)}) copy-start(f32[1024]{0:T(1024)} %get-tuple-element.180) | copy-start | bytes 12292
  277.7 12.2 %copy-start.14 = (f32[1024]{0:T(1024)S(1)}, f32[1024]{0:T(1024)}, u32[]{:S(2)}) copy-start(f32[1024]{0:T(1024)} %get-tuple-element.181) | copy-start | bytes 12292
  277.7 12.2 %copy-start.15 = (f32[1024]{0:T(1024)S(1)}, f32[1024]{0:T(1024)}, u32[]{:S(2)}) copy-start(f32[1024]{0:T(1024)} %get-tuple-element.182) | copy-start | bytes 12292
  277.7 12.2 %copy-start.16 = (f32[1024]{0:T(1024)S(1)}, f32[1024]{0:T(1024)}, u32[]{:S(2)}) copy-start(f32[1024]{0:T(1024)} %get-tuple-element.183) | copy-start | bytes 12292
  277.7 12.2 %copy-start.17 = (f32[1024]{0:T(1024)S(1)}, f32[1024]{0:T(1024)}, u32[]{:S(2)}) copy-start(f32[1024]{0:T(1024)} %get-tuple-element.184) | copy-start | bytes 12292
  277.7 12.2 %copy-start.18 = (f32[1024]{0:T(1024)S(1)}, f32[1024]{0:T(1024)}, u32[]{:S(2)}) copy-start(f32[1024]{0:T(1024)} %get-tuple-element.185) | copy-start | bytes 12292
  277.7 12.2 %copy-start.19 = (f32[1024]{0:T(1024)S(1)}, f32[1024]{0:T(1024)}, u32[]{:S(2)}) copy-start(f32[1024]{0:T(1024)} %get-tuple-element.186) | copy-start | bytes 12292
  277.7 12.2 %copy-start.20 = (f32[1024]{0:T(1024)S(1)}, f32[1024]{0:T(1024)}, u32[]{:S(2)}) copy-start(f32[1024]{0:T(1024)} %get-tuple-element.187) | copy-start | bytes 12292
  277.7 12.2 %copy-start.21 = (f32[1024]{0:T(1024)S(1)}, f32[1024]{0:T(1024)}, u32[]{:S(2)}) copy-start(f32[1024]{0:T(1024)} %get-tuple-element.188) | copy-start | bytes 12292
  277.7 12.2 %copy-start.22 = (f32[1024]{0:T(1024)S(1)}, f32[1024]{0:T(1024)}, u32[]{:S(2)}) copy-start(f32[1024]{0:T(1024)} %get-tuple-element.189) | copy-start | bytes 12292
  277.8 12.2 %copy-start.23 = (f32[1024]{0:T(1024)S(1)}, f32[1024]{0:T(1024)}, u32[]{:S(2)}) copy-start(f32[1024]{0:T(1024)} %get-tuple-element.190) | copy-start | bytes 12292
  277.8 12.2 %copy-start.24 = (f32[1024]{0:T(1024)S(1)}, f32[1024]{0:T(1024)}, u32[]{:S(2)}) copy-start(f32[1024]{0:T(1024)} %get-tuple-element.206) | copy-start | bytes 12292
  279.2 13.5 %copy-start.25 = (f32[1024]{0:T(1024)S(1)}, f32[1024]{0:T(1024)}, u32[]{:S(2)}) copy-start(f32[1024]{0:T(1024)} %get-tuple-element.207) | copy-start | bytes 12292
  281.3 118.7 %all-to-all-start.3 = ((bf16[32,2,6144]{2,1,0:T(2,128)(2,1)}), bf16[32,2,6144]{2,1,0:T(2,128)(2,1)}, u32[]{:S(2)}, u32[]{:S(2)}) async-start(bf16[32,2,6144]{2,1,0:T(2,128)(2,1)} %reshape.158), calls=%async_computation.3 | async-start | bytes 1572864 | tf_op jit(solution)/shard_map/all_to_all | solution.py:29
  287.3 459.9 %all-reduce.2.cloned.1.call-start = ((), (), s32[]{:S(2)}) async-start(), calls=%async_computation.4 | async-start | bytes 262144 | tf_op jit(solution)/shard_map/psum | solution.py:204
  (1 other events, 0.7 us)
Sparse Core Ops, SparseCore 0:
  294.2 452.9 all-reduce.1
where the time goes:
time: 757 us; the launch traced here: 756 us
  waiting for transfers between devices  434 us (57%)
  blocking collectives  107 us (14%)
  starting transfers between devices  72.5 us (10%)
  other arithmetic  47.4 us (6%)
  local copies, waits for them, and re-layouts  44.5 us (6%)
  matrix products  29.9 us (4%)
  between operations  14.7 us (2%)
    psum x1, waiting for transfers between devices, on_device(): grad_kernel, grad_bias = lax.psum((grad_kernel, grad_bias), ('seq', 'dp'))  338 us
    psum x1, blocking collectives, on_device(): grad_kernel, grad_bias = lax.psum((grad_kernel, grad_bias), ('seq', 'dp'))  107 us
    all_to_all x2, waiting for transfers between devices, to_heads(): lax.all_to_all(stacked, 'seq', split_axis=1, concat_axis=0, tiled=True)  72.1 us
    all_to_all x2, starting transfers between devices, to_heads(): lax.all_to_all(stacked, 'seq', split_axis=1, concat_axis=0, tiled=True)  48.5 us
    all_to_all x2, waiting for transfers between devices, to_frames(): lax.all_to_all(stacked, 'seq', split_axis=0, concat_axis=1, tiled=True)  18.8 us
    unnamed x59, local copies, waits for them, and re-layouts  17.6 us
  transfers between devices with their start and end apart: 9, of which 6 were waited for; matrix products, arithmetic and copies ran while one was open for 2% of the time, Pallas kernels for 0%

commit v1 on v0

--- a/solution.py
+++ b/solution.py
@@ -22,7 +22,10 @@
 
 
 def to_heads(stacked):
-    return lax.all_to_all(stacked, "seq", split_axis=1, concat_axis=0, tiled=True)
+    return jnp.concatenate(
+        lax.all_to_all(jnp.stack(jnp.split(stacked, lax.axis_size("seq"), axis=1)), "seq", 0, 0),
+        axis=0,
+    )
 
 
 def to_frames(stacked):

time: 757 us -> 781 us (1.032)
  local copies, waits for them, and re-layouts: 44.5 us -> 66 us
    unnamed x59 -> x119, local copies, waits for them, and re-layouts: 17.6 us -> 36.8 us
where the time goes in v1:
time: 781 us; the launch traced here: 776 us
  waiting for transfers between devices  431 us (55%)
  blocking collectives  107 us (14%)
  starting transfers between devices  74.8 us (10%)
  local copies, waits for them, and re-layouts  66 us (8%)
  other arithmetic  46.5 us (6%)
  matrix products  29.9 us (4%)
  between operations  15.1 us (2%)
    psum x1, waiting for transfers between devices, on_device(): grad_kernel, grad_bias = lax.psum((grad_kernel, grad_bias), ('seq', 'dp'))  337 us
    psum x1, blocking collectives, on_device(): grad_kernel, grad_bias = lax.psum((grad_kernel, grad_bias), ('seq', 'dp'))  107 us
    all_to_all x2, waiting for transfers between devices, to_heads(): lax.all_to_all(jnp.stack(jnp.split(stacked, lax.axis_size('seq'), axis=1)...  70.5 us
    all_to_all x2, starting transfers between devices, to_heads(): lax.all_to_all(jnp.stack(jnp.split(stacked, lax.axis_size('seq'), axis=1)...  47.7 us
    unnamed x119, local copies, waits for them, and re-layouts  36.8 us
    all_to_all x2, waiting for transfers between devices, to_frames(): lax.all_to_all(stacked, 'seq', split_axis=0, concat_axis=1, tiled=True)  19 us
    all_to_all x2, starting transfers between devices, to_frames(): lax.all_to_all(stacked, 'seq', split_axis=0, concat_axis=1, tiled=True)  17.1 us
  transfers between devices with their start and end apart: 9, of which 6 were waited for; matrix products, arithmetic and copies ran while one was open for 2% of the time, Pallas kernels for 0%

profile of v1, /device:TPU:1, one launch (start us, length us, event | category | flops | bytes accessed | tf_op | source)
XLA Modules:
  0.0 776.1 jit_solution(5129795754721421895)
XLA Ops:
  7.2 1.3 reshape.145
  8.5 1.3 reshape.146
  9.8 1.3 reshape.147
  12.6 1.4 fusion.153
  33.4 19.6 %all-to-all-start = ((bf16[32,64,1,192]{3,1,2,0:T(8,128)(2,1)}), bf16[32,64,1,192]{3,1,2,0:T(8,128)(2,1)S(1)}, u32[]{:S(2)}, u32[]{:S(2)}) async-start(bf16[32,64,1,192]{3,1,2,0:T(8,128)(2,1)} %constant_dynamic-update-slice_fusion), calls=%async_computation | async-start | bytes 2097152 | tf_op jit(solution)/shard_map/all_to_all | solution.py:26
  53.7 52.0 %all-to-all-done = bf16[32,64,1,192]{3,1,2,0:T(8,128)(2,1)S(1)} async-done(((bf16[32,64,1,192]{3,1,2,0:T(8,128)(2,1)}), bf16[32,64,1,192]{3,1,2,0:T(8,128)(2,1)S(1)}, u32[]{:S(2)}, u32[]{:S(2)}) %all-to-all-start) | async-done | bytes 786464 | tf_op jit(solution)/shard_map/all_to_all | solution.py:26
  106.1 19.7 %while.41 = (s32[]{:T(128)}, bf16[4,512,64]{1,2,0:T(8,128)(2,1)S(1)}, s32[]{:T(128)}, s32[4]{0:T(128)S(1)}, bf16[2048,64]{1,0:T(8,128)(2,1)S(1)}, /*index=5*/bf1...) while((s32[]{:T(128)}, ...), condition=%wide.region_4.5_spmd, body=%wide.region_1.4_spmd.sunk | while | flops 281052160 | bytes 13846715 | solution.py:63
  109.8 1.3 fusion.188
  114.7 1.3 fusion.188
  127.7 11.6 %reduce.2 = bf16[2048,64]{1,0:T(8,128)(2,1)S(1)} reduce(bf16[2048,1,64]{2,1,0:T(2,128)(2,1)S(1)} %reshape.155, bf16[]{:T(256)} %broadcast.102), dimensions={1}, to_apply=%reshape.155.reduce_sub_computation | reduce | bytes 524290 | tf_op jit(solution)/shard_map/transpose | solution.py:181
  140.4 8.7 %all-to-all-start.1 = ((bf16[32,2,2048]{2,1,0:T(2,128)(2,1)}), bf16[32,2,2048]{2,1,0:T(2,128)(2,1)S(1)}, u32[]{:S(2)}, u32[]{:S(2)}) async-start(bf16[32,2,2048]{2,1,0:T(2,128)(2,1)} %reshape.156), calls=%async_computation.1 | async-start | bytes 524288 | tf_op jit(solution)/shard_map/all_to_all | solution.py:32
  149.3 19.0 %all-to-all-done.1 = bf16[32,2,2048]{2,1,0:T(2,128)(2,1)S(1)} async-done(((bf16[32,2,2048]{2,1,0:T(2,128)(2,1)}), bf16[32,2,2048]{2,1,0:T(2,128)(2,1)S(1)}, u32[]{:S(2)}, u32[]{:S(2)}) %all-to-all-start.1) | async-done | bytes 262176 | tf_op jit(solution)/shard_map/all_to_all | solution.py:32
  169.9 2.0 copy.1794
  171.9 1.7 reshape.153
  173.9 1.9 collective-permute-start
  175.9 2.4 collective-permute-start.1
  178.3 3.1 collective-permute-done.1
  181.4 5.0 fusion.89
  187.6 1.9 collective-permute-start.2
  189.5 3.6 collective-permute-start.3
  193.2 1.3 collective-permute-done.3
  194.5 3.3 fusion.91
  198.8 1.3 reshape.148
  202.9 28.1 %all-to-all-start.2 = ((bf16[32,2,2048]{2,1,0:T(2,128)(2,1)}), bf16[32,2,2048]{2,1,0:T(2,128)(2,1)}, u32[]{:S(2)}, u32[]{:S(2)}) async-start(bf16[32,2,2048]{2,1,0:T(2,128)(2,1)} %reshape.158), calls=%async_computation.2 | async-start | bytes 524288 | tf_op jit(solution)/shard_map/all_to_all | solution.py:26
  231.0 18.4 %all-to-all-done.2 = bf16[32,2,2048]{2,1,0:T(2,128)(2,1)} async-done(((bf16[32,2,2048]{2,1,0:T(2,128)(2,1)}), bf16[32,2,2048]{2,1,0:T(2,128)(2,1)}, u32[]{:S(2)}, u32[]{:S(2)}) %all-to-all-start.2) | async-done | bytes 262176 | tf_op jit(solution)/shard_map/all_to_all | solution.py:26
  249.5 2.1 reshape.159
  252.3 40.2 %while.42 = (s32[]{:T(128)}, f32[2048,64]{0,1:T(8,128)S(1)}, f32[2048,64]{0,1:T(8,128)}, bf16[4,512,64]{1,2,0:T(8,128)(2,1)}, s32[]{:T(128)}, /*index=5*/s32[4]{...) while((s32[]{:T(128)}, f32[2048,64]{0,1:T(8,128)S(1)}, ...), condition=%wide.region_9.10_spmd.clone, body=%wide.region_5.9_spmd.clone.sunk | while | flops 698909184 | bytes 45975896 | solution.py:96
  257.2 1.4 multiply_reduce_fusion.2
  258.7 1.7 multiply_convert_fusion.2
  260.4 1.4 fusion.199
  267.3 1.4 multiply_reduce_fusion.2
  268.7 1.7 multiply_convert_fusion.2
  270.4 1.4 fusion.199
  277.4 1.4 multiply_reduce_fusion.2
  278.8 1.7 multiply_convert_fusion.2
  280.5 1.4 fusion.199
  287.4 1.4 multiply_reduce_fusion.2
  288.9 1.7 multiply_convert_fusion.2
  290.5 1.4 fusion.199
  294.7 1.9 reduce.3
  296.8 1.4 copy.1947
  298.2 2.1 reshape.160
  300.3 8.4 %all-to-all-start.3 = ((bf16[32,2,6144]{2,1,0:T(2,128)(2,1)}), bf16[32,2,6144]{2,1,0:T(2,128)(2,1)}, u32[]{:S(2)}, u32[]{:S(2)}) async-start(bf16[32,2,6144]{2,1,0:T(2,128)(2,1)} %reshape.160), calls=%async_computation.3 | async-start | bytes 1572864 | tf_op jit(solution)/shard_map/all_to_all | solution.py:32
  311.4 2.7 stack.391
  314.1 107.5 %psum.15 = f32[1024]{0:T(1024)} all-reduce(f32[1024]{0:T(1024)S(1)} %copy-done.24), channel_id=1, replica_groups=mesh['seq'=32,'dp'=16] {'seq','dp'}, use_global_device_ids=true, to_apply=%region_43.44 | all-reduce | flops 1024 | bytes 8192 | tf_op jit(solution)/shard_map/psum | solution.py:207
  421.6 4.5 reshape.161
  430.7 336.7 %all-reduce.2.cloned.1.call-done = f32[31,1024]{1,0:T(8,128)} async-done(((f32[31,1024]{1,0:T(8,128)}), f32[31,1024]{1,0:T(8,128)}) %all-reduce.2.cloned.1.call-update) | async-done | bytes 126992 | tf_op jit(solution)/shard_map/psum | solution.py:207
  767.4 1.6 copy.2031
  (234 shorter events, 75.3 us)
Async XLA Ops:
  12.6 40.5 %copy-start.26 = (s32[2]{0:T(128)S(1)}, s32[2]{0:T(128)}, u32[]{:S(2)}) copy-start(s32[2]{0:T(128)} %param.17) | copy-start | bytes 28
  33.4 72.3 %all-to-all-start = ((bf16[32,64,1,192]{3,1,2,0:T(8,128)(2,1)}), bf16[32,64,1,192]{3,1,2,0:T(8,128)(2,1)S(1)}, u32[]{:S(2)}, u32[]{:S(2)}) async-start(bf16[32,64,1,192]{3,1,2,0:T(8,128)(2,1)} %constant_dynamic-update-slice_fusion), calls=%async_computation | async-start | bytes 2097152 | tf_op jit(solution)/shard_map/all_to_all | solution.py:26
  125.8 0.8 copy-start.6
  126.6 22.6 %copy-start.8 = (f32[31,1024]{1,0:T(8,128)S(1)}, f32[31,1024]{1,0:T(8,128)}, u32[]{:S(2)}) copy-start(f32[31,1024]{1,0:T(8,128)} %param.18) | copy-start | bytes 380932
  140.4 33.3 %copy-start.1 = (bf16[64,2,1024]{2,1,0:T(2,128)(2,1)S(1)}, bf16[64,2,1024]{2,1,0:T(2,128)(2,1)}, u32[]{:S(2)}) copy-start(bf16[64,2,1024]{2,1,0:T(2,128)(2,1)} %param.15) | copy-start | bytes 786436
  140.4 27.9 %all-to-all-start.1 = ((bf16[32,2,2048]{2,1,0:T(2,128)(2,1)}), bf16[32,2,2048]{2,1,0:T(2,128)(2,1)S(1)}, u32[]{:S(2)}, u32[]{:S(2)}) async-start(bf16[32,2,2048]{2,1,0:T(2,128)(2,1)} %reshape.156), calls=%async_computation.1 | async-start | bytes 524288 | tf_op jit(solution)/shard_map/all_to_all | solution.py:32
  149.2 24.4 %copy-start.25 = (pred[64,2]{0,1:T(4,128)(4,1)}, pred[64,2]{0,1:T(4,128)(4,1)S(1)}, u32[]{:S(2)}) copy-start(pred[64,2]{0,1:T(4,128)(4,1)S(1)} %broadcast_compare_fusion) | copy-start | bytes 388
  168.9 12.6 %copy-start = (bf16[64,2,1024]{2,1,0:T(2,128)(2,1)S(1)}, bf16[64,2,1024]{2,1,0:T(2,128)(2,1)}, u32[]{:S(2)}) copy-start(bf16[64,2,1024]{2,1,0:T(2,128)(2,1)} %param.16) | copy-start | bytes 786436
  173.9 4.4 collective-permute-start
  175.9 5.6 collective-permute-start.1
  187.6 5.6 collective-permute-start.2
  189.5 5.0 collective-permute-start.3
  202.9 46.6 %all-to-all-start.2 = ((bf16[32,2,2048]{2,1,0:T(2,128)(2,1)}), bf16[32,2,2048]{2,1,0:T(2,128)(2,1)}, u32[]{:S(2)}, u32[]{:S(2)}) async-start(bf16[32,2,2048]{2,1,0:T(2,128)(2,1)} %reshape.158), calls=%async_computation.2 | async-start | bytes 524288 | tf_op jit(solution)/shard_map/all_to_all | solution.py:26
  254.2 1.8 copy-start.3
  254.2 1.8 copy-start.4
  256.0 1.2 copy-start.7
  257.2 1.4 copy-start.5
  264.3 1.8 copy-start.3
  264.3 1.8 copy-start.4
  266.0 1.2 copy-start.7
  267.3 1.4 copy-start.5
  274.3 1.8 copy-start.3
  274.3 1.8 copy-start.4
  276.1 1.2 copy-start.7
  277.3 1.4 copy-start.5
  284.4 1.8 copy-start.3
  284.4 1.8 copy-start.4
  286.1 1.2 copy-start.7
  287.4 1.4 copy-start.5
  294.7 14.1 %copy-start.2 = (bf16[64,2,1024]{2,1,0:T(2,128)(2,1)S(1)}, bf16[64,2,1024]{2,1,0:T(2,128)(2,1)}, u32[]{:S(2)}) copy-start(bf16[64,2,1024]{2,1,0:T(2,128)(2,1)} %param.15) | copy-start | bytes 786436
  296.6 14.6 %copy-start.9 = (f32[1024]{0:T(1024)S(1)}, f32[1024]{0:T(1024)}, u32[]{:S(2)}) copy-start(f32[1024]{0:T(1024)} %get-tuple-element.170) | copy-start | bytes 12292
  296.6 14.6 %copy-start.10 = (f32[1024]{0:T(1024)S(1)}, f32[1024]{0:T(1024)}, u32[]{:S(2)}) copy-start(f32[1024]{0:T(1024)} %get-tuple-element.171) | copy-start | bytes 12292
  296.6 14.6 %copy-start.11 = (f32[1024]{0:T(1024)S(1)}, f32[1024]{0:T(1024)}, u32[]{:S(2)}) copy-start(f32[1024]{0:T(1024)} %get-tuple-element.172) | copy-start | bytes 12292
  296.6 14.6 %copy-start.12 = (f32[1024]{0:T(1024)S(1)}, f32[1024]{0:T(1024)}, u32[]{:S(2)}) copy-start(f32[1024]{0:T(1024)} %get-tuple-element.173) | copy-start | bytes 12292
  296.7 14.6 %copy-start.13 = (f32[1024]{0:T(1024)S(1)}, f32[1024]{0:T(1024)}, u32[]{:S(2)}) copy-start(f32[1024]{0:T(1024)} %get-tuple-element.174) | copy-start | bytes 12292
  296.7 14.6 %copy-start.14 = (f32[1024]{0:T(1024)S(1)}, f32[1024]{0:T(1024)}, u32[]{:S(2)}) copy-start(f32[1024]{0:T(1024)} %get-tuple-element.175) | copy-start | bytes 12292
  296.7 14.6 %copy-start.15 = (f32[1024]{0:T(1024)S(1)}, f32[1024]{0:T(1024)}, u32[]{:S(2)}) copy-start(f32[1024]{0:T(1024)} %get-tuple-element.176) | copy-start | bytes 12292
  296.7 14.6 %copy-start.16 = (f32[1024]{0:T(1024)S(1)}, f32[1024]{0:T(1024)}, u32[]{:S(2)}) copy-start(f32[1024]{0:T(1024)} %get-tuple-element.177) | copy-start | bytes 12292
  296.7 14.6 %copy-start.17 = (f32[1024]{0:T(1024)S(1)}, f32[1024]{0:T(1024)}, u32[]{:S(2)}) copy-start(f32[1024]{0:T(1024)} %get-tuple-element.178) | copy-start | bytes 12292
  296.7 14.6 %copy-start.18 = (f32[1024]{0:T(1024)S(1)}, f32[1024]{0:T(1024)}, u32[]{:S(2)}) copy-start(f32[1024]{0:T(1024)} %get-tuple-element.179) | copy-start | bytes 12292
  296.7 14.6 %copy-start.19 = (f32[1024]{0:T(1024)S(1)}, f32[1024]{0:T(1024)}, u32[]{:S(2)}) copy-start(f32[1024]{0:T(1024)} %get-tuple-element.180) | copy-start | bytes 12292
  296.7 14.6 %copy-start.20 = (f32[1024]{0:T(1024)S(1)}, f32[1024]{0:T(1024)}, u32[]{:S(2)}) copy-start(f32[1024]{0:T(1024)} %get-tuple-element.181) | copy-start | bytes 12292
  296.7 14.6 %copy-start.21 = (f32[1024]{0:T(1024)S(1)}, f32[1024]{0:T(1024)}, u32[]{:S(2)}) copy-start(f32[1024]{0:T(1024)} %get-tuple-element.182) | copy-start | bytes 12292
  296.7 14.6 %copy-start.22 = (f32[1024]{0:T(1024)S(1)}, f32[1024]{0:T(1024)}, u32[]{:S(2)}) copy-start(f32[1024]{0:T(1024)} %get-tuple-element.183) | copy-start | bytes 12292
  296.7 14.6 %copy-start.23 = (f32[1024]{0:T(1024)S(1)}, f32[1024]{0:T(1024)}, u32[]{:S(2)}) copy-start(f32[1024]{0:T(1024)} %get-tuple-element.199) | copy-start | bytes 12292
  298.2 15.9 %copy-start.24 = (f32[1024]{0:T(1024)S(1)}, f32[1024]{0:T(1024)}, u32[]{:S(2)}) copy-start(f32[1024]{0:T(1024)} %get-tuple-element.200) | copy-start | bytes 12292
  300.3 121.3 %all-to-all-start.3 = ((bf16[32,2,6144]{2,1,0:T(2,128)(2,1)}), bf16[32,2,6144]{2,1,0:T(2,128)(2,1)}, u32[]{:S(2)}, u32[]{:S(2)}) async-start(bf16[32,2,6144]{2,1,0:T(2,128)(2,1)} %reshape.160), calls=%async_computation.3 | async-start | bytes 1572864 | tf_op jit(solution)/shard_map/all_to_all | solution.py:32
  308.7 458.7 %all-reduce.2.cloned.1.call-start = ((), (), s32[]{:S(2)}) async-start(), calls=%async_computation.4 | async-start | bytes 262144 | tf_op jit(solution)/shard_map/psum | solution.py:207
Sparse Core Ops, SparseCore 0:
  315.6 451.7 all-reduce.1
